TPU v7x, 32 devices: a whole 2x2x4 slice. The times are simulated.
32 devices in a mesh: grp: 2 (over y), tm: 16 (over z, x, core).
Axes of the slice: x: 2, y: 2, z: 4, core: 2. Of those that a mesh axis runs over, the one named last changes fastest.
Arguments:
- residual: bfloat16 [4, 2, 4096, 2048], P('grp', None, 'tm'), parts along dimension 0, may hold values from -6 to 6
- eigenbasis: bfloat16 [2048, 2048], P('tm'), may hold values from -0.125 to 0.125
- eigenvalues: float32 [2048], replicated, may hold values from 0.05 to 5
- node_order: int32 [2048], replicated, may hold values from 0 to 2047, each once
Outputs:
- correction: float32 [4, 2, 4096, 2048], P('grp', None, 'tm'), parts along dimension 0
There are 2 independent parts, one for each index of `grp`. A program takes and returns all parts, laid end to end along the dimension named above; an argument that names none is the same for every part. Nothing has to cross between parts.
Inputs may be any that keep to these rules, and one draw needn't show every extreme that they name: node_order names every number of 0 to 2047 exactly once.
All inputs are finite; a program needn't handle non-finite values.
Results may differ from a plain program's by a relative error of at most 0.0055.
Values may be sent and summed in bfloat16 or wider, within the bound.
A program may use at most 64 MiB of HBM per device.

v0:
```python
import jax
import jax.numpy as jnp
from jax import lax
from jax.sharding import PartitionSpec as P


def sine_block(length, first_col, block_width):
    row_index = jnp.arange(length, dtype=jnp.int32)[:, None] + 1
    col_index = first_col + jnp.arange(block_width, dtype=jnp.int32)[None, :] + 1
    phase_mod = row_index * col_index % (2 * (length + 1))
    angle_rad = phase_mod.astype(jnp.float32) * (jnp.pi / (length + 1))
    return (jnp.sqrt(2.0 / (length + 1)) * jnp.sin(angle_rad)).astype(jnp.bfloat16)


def on_device(residual, eigenbasis, eigenvalues, node_order):
    num_vectors, fields, time_local, states = residual.shape
    length = time_local * lax.axis_size("tm")
    inverse = jnp.zeros_like(node_order).at[node_order].set(jnp.arange(states, dtype=jnp.int32))
    ordered = jnp.take(residual, node_order, axis=3)
    modal_data = jnp.einsum(
        "sj,rfts->rftj",
        lax.all_gather(eigenbasis, "tm", axis=0, tiled=True),
        ordered,
        preferred_element_type=jnp.float32,
    ).astype(jnp.bfloat16)
    spread = lax.all_to_all(modal_data, "tm", split_axis=3, concat_axis=2, tiled=True)
    mode_count = spread.shape[3]
    offset = lax.axis_index("tm") * mode_count
    local_mu = lax.dynamic_slice_in_dim(eigenvalues, offset, mode_count, 0)
    block_width = min(256, length)

    def one_block(block_index, accumulated):
        first_col = block_index * block_width
        sine_table = sine_block(length, first_col, block_width)
        spectral = jnp.einsum(
            "rftj,tk->rfjk", spread, sine_table, preferred_element_type=jnp.float32
        )
        freq_index = (first_col + jnp.arange(block_width, dtype=jnp.int32) + 1).astype(jnp.float32)
        time_eigen = 4.0 * jnp.sin(freq_index * (jnp.pi / (2 * (length + 1)))) ** 2
        shift_sum = local_mu[:, None] + time_eigen[None, :]
        determinant = shift_sum * shift_sum + 1.0
        state_part = (shift_sum * spectral[:, 0] - spectral[:, 1]) / determinant
        adjoint = (spectral[:, 0] + shift_sum * spectral[:, 1]) / determinant
        scaled = jnp.stack((state_part, adjoint), axis=1).astype(jnp.bfloat16)
        return accumulated + jnp.einsum(
            "rfjk,tk->rfjt", scaled, sine_table, preferred_element_type=jnp.float32
        )

    zero_modes = jnp.zeros((num_vectors, fields, mode_count, length), jnp.float32)
    accumulated = lax.fori_loop(0, length // block_width, one_block, zero_modes)
    back_modes = accumulated.astype(jnp.bfloat16)
    returned = lax.all_to_all(back_modes, "tm", split_axis=3, concat_axis=2, tiled=True)
    shaped = jnp.einsum(
        "sj,rfjt->rfts",
        lax.all_gather(eigenbasis, "tm", axis=0, tiled=True),
        returned,
        preferred_element_type=jnp.float32,
    )
    return jnp.take(shaped, inverse, axis=3)


def solution(mesh):
    placed = (P("grp", None, "tm", None), P("tm", None), P(), P())
    return jax.shard_map(
        on_device, mesh=mesh, in_specs=placed, out_specs=P("grp", None, "tm", None), check_vma=False
    )
```

profile of v0, /device:TPU:11, one launch (start us, length us, event | category | flops | bytes accessed | tf_op | source)
XLA Modules:
  0.0 1137.6 jit_solution(11743297354848499549)
XLA Ops:
  7.3 11.1 copy.19
  18.4 24.5 %gather_fusion = bf16[2048,2,2,256]{3,2,1,0:T(2,128)(2,1)} fusion(bf16[2,2,256,2048]{2,1,3,0:T(2,128)(2,1)} %copy.19, s32[2048]{0:T(1024)S(1)} %get-tuple-element.145), kind=kCustom, calls=%fused_computation | custom fusion | bytes 8396800 | tf_op jit(solution)/shard_map/jit(_take)/gather | solution.py:19
  42.9 9.3 fusion.38
  52.2 32.3 %all-gather.2.cloned.1.call-done = bf16[2048,2048]{1,0:T(8,128)(2,1)} async-done(((bf16[128,2048]{1,0:T(8,128)(2,1)}), bf16[2048,2048]{1,0:T(8,128)(2,1)}) %all-gather.2.cloned.1.call-update) | async-done | bytes 8388624 | tf_op jit(solution)/shard_map/all_gather | solution.py:22
  84.5 14.1 %fusion.39 = bf16[2,2,256,2048]{3,2,1,0:T(8,128)(2,1)} fusion(bf16[2048,2048]{1,0:T(8,128)(2,1)} %all-gather.2.cloned.1.call-done, bf16[2,2,256,2048]{2,1,0,3:T(2,128)(2,1)} %fusion.38), kind=kOutput, calls=%fused_computation.51 | convolution fusion | flops 8592031744 | bytes 16777216 | tf_op jit(solution)/shard_map/sj,rfts->rftj/dot_general | solution.py:20
  98.6 11.2 copy.21
  116.8 91.7 %all-to-all-done = bf16[2,2,256,2048]{2,1,0,3:T(2,128)(2,1)} async-done(((bf16[2,2,256,2048]{2,1,0,3:T(2,128)(2,1)}), bf16[2,2,256,2048]{2,1,0,3:T(2,128)(2,1)}, u32[]{:S(2)}, u32[]{:S(2)}) %all-to-all-start) | async-done | bytes 4194336 | tf_op jit(solution)/shard_map/all_to_all | solution.py:26
  208.5 11.1 copy.22
  219.6 709.7 %while.16 = (s32[]{:T(128)}, f32[2,2,128,4096]{3,2,1,0:T(8,128)}, f32[128]{0:T(128)S(1)}, bf16[2,2,4096,128]{3,2,1,0:T(8,128)(2,1)}, s32[]{:T(128)}, /*index=5*/s32[]{:T(128)}, s32[]{:T(128)}) while((s32[]{:T(128)}, f32[2,2,128,4096]{3,2,1,0:T(8,128)}, f32[128]{0:T(128)S(1)}, bf16[2,2,4096,128]{3,2,1,0:T(8,128)(2,1)}, s32[]{:T(128)}, ...), condition=%wide.region_2.3_spmd.clone, body=%wide.region_1.2_spmd.clone.sunk | while | flops 2175506432 | bytes 23123560 | solution.py:50
  219.6 22.2 %fusion.58 = f32[2,2,128,256]{2,3,1,0:T(8,128)S(1)} fusion(bf16[2,2,4096,128]{3,2,1,0:T(8,128)(2,1)} %get-tuple-element.196, s32[256]{0:T(256)S(1)} %add_add_fusion.2, s32[4096]{0:T(1024)S(1)} %iota_add_fusion.2), kind=kOutput, calls=%fused_computation.22.clone.1 | convolution fusion | flops 1085276160 | bytes 4736000 | tf_op jit(solution)/shard_map/while/body/eval_jaxpr/rftj,tk->rfjk/dot_general | solution.py:35
  242.1 20.8 %select_add_fusion.2 = f32[2,2,128,4096]{3,2,1,0:T(8,128)} fusion(f32[2,2,128,4096]{3,2,1,0:T(8,128)} %get-tuple-element.187, pred[]{:T(512)S(6)} %compare.3, s32[256]{0:T(256)S(1)} %add_add_fusion.2, s32[4096]{0:T(1024)S(1)} %iota_add_fusion.2, bf16[2,1,128,256]{2,3,1,0:T(8,128)(2,1)S(1)} %get-tuple-element.177, ...), kind=kOutput, calls=%fused_computation.3.clone.1 | convolution fusion | flops 1089601536 | bytes 17056768 | tf_op jit(solution)/shard_map/while/body/eval_jaxpr/rfjk,tk->rfjt/dot_general | solution.py:45
  262.9 22.2 %fusion.58 = f32[2,2,128,256]{2,3,1,0:T(8,128)S(1)} fusion(bf16[2,2,4096,128]{3,2,1,0:T(8,128)(2,1)} %get-tuple-element.196, s32[256]{0:T(256)S(1)} %add_add_fusion.2, s32[4096]{0:T(1024)S(1)} %iota_add_fusion.2), kind=kOutput, calls=%fused_computation.22.clone.1 | convolution fusion | flops 1085276160 | bytes 4736000 | tf_op jit(solution)/shard_map/while/body/eval_jaxpr/rftj,tk->rfjk/dot_general | solution.py:35
  285.3 22.0 %select_add_fusion.2 = f32[2,2,128,4096]{3,2,1,0:T(8,128)} fusion(f32[2,2,128,4096]{3,2,1,0:T(8,128)} %get-tuple-element.187, pred[]{:T(512)S(6)} %compare.3, s32[256]{0:T(256)S(1)} %add_add_fusion.2, s32[4096]{0:T(1024)S(1)} %iota_add_fusion.2, bf16[2,1,128,256]{2,3,1,0:T(8,128)(2,1)S(1)} %get-tuple-element.177, ...), kind=kOutput, calls=%fused_computation.3.clone.1 | convolution fusion | flops 1089601536 | bytes 17056768 | tf_op jit(solution)/shard_map/while/body/eval_jaxpr/rfjk,tk->rfjt/dot_general | solution.py:45
  307.3 22.2 %fusion.58 = f32[2,2,128,256]{2,3,1,0:T(8,128)S(1)} fusion(bf16[2,2,4096,128]{3,2,1,0:T(8,128)(2,1)} %get-tuple-element.196, s32[256]{0:T(256)S(1)} %add_add_fusion.2, s32[4096]{0:T(1024)S(1)} %iota_add_fusion.2), kind=kOutput, calls=%fused_computation.22.clone.1 | convolution fusion | flops 1085276160 | bytes 4736000 | tf_op jit(solution)/shard_map/while/body/eval_jaxpr/rftj,tk->rfjk/dot_general | solution.py:35
  329.8 22.0 %select_add_fusion.2 = f32[2,2,128,4096]{3,2,1,0:T(8,128)} fusion(f32[2,2,128,4096]{3,2,1,0:T(8,128)} %get-tuple-element.187, pred[]{:T(512)S(6)} %compare.3, s32[256]{0:T(256)S(1)} %add_add_fusion.2, s32[4096]{0:T(1024)S(1)} %iota_add_fusion.2, bf16[2,1,128,256]{2,3,1,0:T(8,128)(2,1)S(1)} %get-tuple-element.177, ...), kind=kOutput, calls=%fused_computation.3.clone.1 | convolution fusion | flops 1089601536 | bytes 17056768 | tf_op jit(solution)/shard_map/while/body/eval_jaxpr/rfjk,tk->rfjt/dot_general | solution.py:45
  351.7 22.2 %fusion.58 = f32[2,2,128,256]{2,3,1,0:T(8,128)S(1)} fusion(bf16[2,2,4096,128]{3,2,1,0:T(8,128)(2,1)} %get-tuple-element.196, s32[256]{0:T(256)S(1)} %add_add_fusion.2, s32[4096]{0:T(1024)S(1)} %iota_add_fusion.2), kind=kOutput, calls=%fused_computation.22.clone.1 | convolution fusion | flops 1085276160 | bytes 4736000 | tf_op jit(solution)/shard_map/while/body/eval_jaxpr/rftj,tk->rfjk/dot_general | solution.py:35
  374.2 22.0 %select_add_fusion.2 = f32[2,2,128,4096]{3,2,1,0:T(8,128)} fusion(f32[2,2,128,4096]{3,2,1,0:T(8,128)} %get-tuple-element.187, pred[]{:T(512)S(6)} %compare.3, s32[256]{0:T(256)S(1)} %add_add_fusion.2, s32[4096]{0:T(1024)S(1)} %iota_add_fusion.2, bf16[2,1,128,256]{2,3,1,0:T(8,128)(2,1)S(1)} %get-tuple-element.177, ...), kind=kOutput, calls=%fused_computation.3.clone.1 | convolution fusion | flops 1089601536 | bytes 17056768 | tf_op jit(solution)/shard_map/while/body/eval_jaxpr/rfjk,tk->rfjt/dot_general | solution.py:45
  396.1 22.2 %fusion.58 = f32[2,2,128,256]{2,3,1,0:T(8,128)S(1)} fusion(bf16[2,2,4096,128]{3,2,1,0:T(8,128)(2,1)} %get-tuple-element.196, s32[256]{0:T(256)S(1)} %add_add_fusion.2, s32[4096]{0:T(1024)S(1)} %iota_add_fusion.2), kind=kOutput, calls=%fused_computation.22.clone.1 | convolution fusion | flops 1085276160 | bytes 4736000 | tf_op jit(solution)/shard_map/while/body/eval_jaxpr/rftj,tk->rfjk/dot_general | solution.py:35
  418.6 22.0 %select_add_fusion.2 = f32[2,2,128,4096]{3,2,1,0:T(8,128)} fusion(f32[2,2,128,4096]{3,2,1,0:T(8,128)} %get-tuple-element.187, pred[]{:T(512)S(6)} %compare.3, s32[256]{0:T(256)S(1)} %add_add_fusion.2, s32[4096]{0:T(1024)S(1)} %iota_add_fusion.2, bf16[2,1,128,256]{2,3,1,0:T(8,128)(2,1)S(1)} %get-tuple-element.177, ...), kind=kOutput, calls=%fused_computation.3.clone.1 | convolution fusion | flops 1089601536 | bytes 17056768 | tf_op jit(solution)/shard_map/while/body/eval_jaxpr/rfjk,tk->rfjt/dot_general | solution.py:45
  440.6 22.2 %fusion.58 = f32[2,2,128,256]{2,3,1,0:T(8,128)S(1)} fusion(bf16[2,2,4096,128]{3,2,1,0:T(8,128)(2,1)} %get-tuple-element.196, s32[256]{0:T(256)S(1)} %add_add_fusion.2, s32[4096]{0:T(1024)S(1)} %iota_add_fusion.2), kind=kOutput, calls=%fused_computation.22.clone.1 | convolution fusion | flops 1085276160 | bytes 4736000 | tf_op jit(solution)/shard_map/while/body/eval_jaxpr/rftj,tk->rfjk/dot_general | solution.py:35
  463.0 22.0 %select_add_fusion.2 = f32[2,2,128,4096]{3,2,1,0:T(8,128)} fusion(f32[2,2,128,4096]{3,2,1,0:T(8,128)} %get-tuple-element.187, pred[]{:T(512)S(6)} %compare.3, s32[256]{0:T(256)S(1)} %add_add_fusion.2, s32[4096]{0:T(1024)S(1)} %iota_add_fusion.2, bf16[2,1,128,256]{2,3,1,0:T(8,128)(2,1)S(1)} %get-tuple-element.177, ...), kind=kOutput, calls=%fused_computation.3.clone.1 | convolution fusion | flops 1089601536 | bytes 17056768 | tf_op jit(solution)/shard_map/while/body/eval_jaxpr/rfjk,tk->rfjt/dot_general | solution.py:45
  485.0 22.2 %fusion.58 = f32[2,2,128,256]{2,3,1,0:T(8,128)S(1)} fusion(bf16[2,2,4096,128]{3,2,1,0:T(8,128)(2,1)} %get-tuple-element.196, s32[256]{0:T(256)S(1)} %add_add_fusion.2, s32[4096]{0:T(1024)S(1)} %iota_add_fusion.2), kind=kOutput, calls=%fused_computation.22.clone.1 | convolution fusion | flops 1085276160 | bytes 4736000 | tf_op jit(solution)/shard_map/while/body/eval_jaxpr/rftj,tk->rfjk/dot_general | solution.py:35
  507.5 22.0 %select_add_fusion.2 = f32[2,2,128,4096]{3,2,1,0:T(8,128)} fusion(f32[2,2,128,4096]{3,2,1,0:T(8,128)} %get-tuple-element.187, pred[]{:T(512)S(6)} %compare.3, s32[256]{0:T(256)S(1)} %add_add_fusion.2, s32[4096]{0:T(1024)S(1)} %iota_add_fusion.2, bf16[2,1,128,256]{2,3,1,0:T(8,128)(2,1)S(1)} %get-tuple-element.177, ...), kind=kOutput, calls=%fused_computation.3.clone.1 | convolution fusion | flops 1089601536 | bytes 17056768 | tf_op jit(solution)/shard_map/while/body/eval_jaxpr/rfjk,tk->rfjt/dot_general | solution.py:45
  529.4 22.2 %fusion.58 = f32[2,2,128,256]{2,3,1,0:T(8,128)S(1)} fusion(bf16[2,2,4096,128]{3,2,1,0:T(8,128)(2,1)} %get-tuple-element.196, s32[256]{0:T(256)S(1)} %add_add_fusion.2, s32[4096]{0:T(1024)S(1)} %iota_add_fusion.2), kind=kOutput, calls=%fused_computation.22.clone.1 | convolution fusion | flops 1085276160 | bytes 4736000 | tf_op jit(solution)/shard_map/while/body/eval_jaxpr/rftj,tk->rfjk/dot_general | solution.py:35
  551.9 22.0 %select_add_fusion.2 = f32[2,2,128,4096]{3,2,1,0:T(8,128)} fusion(f32[2,2,128,4096]{3,2,1,0:T(8,128)} %get-tuple-element.187, pred[]{:T(512)S(6)} %compare.3, s32[256]{0:T(256)S(1)} %add_add_fusion.2, s32[4096]{0:T(1024)S(1)} %iota_add_fusion.2, bf16[2,1,128,256]{2,3,1,0:T(8,128)(2,1)S(1)} %get-tuple-element.177, ...), kind=kOutput, calls=%fused_computation.3.clone.1 | convolution fusion | flops 1089601536 | bytes 17056768 | tf_op jit(solution)/shard_map/while/body/eval_jaxpr/rfjk,tk->rfjt/dot_general | solution.py:45
  573.9 22.2 %fusion.58 = f32[2,2,128,256]{2,3,1,0:T(8,128)S(1)} fusion(bf16[2,2,4096,128]{3,2,1,0:T(8,128)(2,1)} %get-tuple-element.196, s32[256]{0:T(256)S(1)} %add_add_fusion.2, s32[4096]{0:T(1024)S(1)} %iota_add_fusion.2), kind=kOutput, calls=%fused_computation.22.clone.1 | convolution fusion | flops 1085276160 | bytes 4736000 | tf_op jit(solution)/shard_map/while/body/eval_jaxpr/rftj,tk->rfjk/dot_general | solution.py:35
  596.3 22.0 %select_add_fusion.2 = f32[2,2,128,4096]{3,2,1,0:T(8,128)} fusion(f32[2,2,128,4096]{3,2,1,0:T(8,128)} %get-tuple-element.187, pred[]{:T(512)S(6)} %compare.3, s32[256]{0:T(256)S(1)} %add_add_fusion.2, s32[4096]{0:T(1024)S(1)} %iota_add_fusion.2, bf16[2,1,128,256]{2,3,1,0:T(8,128)(2,1)S(1)} %get-tuple-element.177, ...), kind=kOutput, calls=%fused_computation.3.clone.1 | convolution fusion | flops 1089601536 | bytes 17056768 | tf_op jit(solution)/shard_map/while/body/eval_jaxpr/rfjk,tk->rfjt/dot_general | solution.py:45
  618.3 22.2 %fusion.58 = f32[2,2,128,256]{2,3,1,0:T(8,128)S(1)} fusion(bf16[2,2,4096,128]{3,2,1,0:T(8,128)(2,1)} %get-tuple-element.196, s32[256]{0:T(256)S(1)} %add_add_fusion.2, s32[4096]{0:T(1024)S(1)} %iota_add_fusion.2), kind=kOutput, calls=%fused_computation.22.clone.1 | convolution fusion | flops 1085276160 | bytes 4736000 | tf_op jit(solution)/shard_map/while/body/eval_jaxpr/rftj,tk->rfjk/dot_general | solution.py:35
  640.8 22.0 %select_add_fusion.2 = f32[2,2,128,4096]{3,2,1,0:T(8,128)} fusion(f32[2,2,128,4096]{3,2,1,0:T(8,128)} %get-tuple-element.187, pred[]{:T(512)S(6)} %compare.3, s32[256]{0:T(256)S(1)} %add_add_fusion.2, s32[4096]{0:T(1024)S(1)} %iota_add_fusion.2, bf16[2,1,128,256]{2,3,1,0:T(8,128)(2,1)S(1)} %get-tuple-element.177, ...), kind=kOutput, calls=%fused_computation.3.clone.1 | convolution fusion | flops 1089601536 | bytes 17056768 | tf_op jit(solution)/shard_map/while/body/eval_jaxpr/rfjk,tk->rfjt/dot_general | solution.py:45
  662.7 22.2 %fusion.58 = f32[2,2,128,256]{2,3,1,0:T(8,128)S(1)} fusion(bf16[2,2,4096,128]{3,2,1,0:T(8,128)(2,1)} %get-tuple-element.196, s32[256]{0:T(256)S(1)} %add_add_fusion.2, s32[4096]{0:T(1024)S(1)} %iota_add_fusion.2), kind=kOutput, calls=%fused_computation.22.clone.1 | convolution fusion | flops 1085276160 | bytes 4736000 | tf_op jit(solution)/shard_map/while/body/eval_jaxpr/rftj,tk->rfjk/dot_general | solution.py:35
  685.2 22.0 %select_add_fusion.2 = f32[2,2,128,4096]{3,2,1,0:T(8,128)} fusion(f32[2,2,128,4096]{3,2,1,0:T(8,128)} %get-tuple-element.187, pred[]{:T(512)S(6)} %compare.3, s32[256]{0:T(256)S(1)} %add_add_fusion.2, s32[4096]{0:T(1024)S(1)} %iota_add_fusion.2, bf16[2,1,128,256]{2,3,1,0:T(8,128)(2,1)S(1)} %get-tuple-element.177, ...), kind=kOutput, calls=%fused_computation.3.clone.1 | convolution fusion | flops 1089601536 | bytes 17056768 | tf_op jit(solution)/shard_map/while/body/eval_jaxpr/rfjk,tk->rfjt/dot_general | solution.py:45
  707.2 22.2 %fusion.58 = f32[2,2,128,256]{2,3,1,0:T(8,128)S(1)} fusion(bf16[2,2,4096,128]{3,2,1,0:T(8,128)(2,1)} %get-tuple-element.196, s32[256]{0:T(256)S(1)} %add_add_fusion.2, s32[4096]{0:T(1024)S(1)} %iota_add_fusion.2), kind=kOutput, calls=%fused_computation.22.clone.1 | convolution fusion | flops 1085276160 | bytes 4736000 | tf_op jit(solution)/shard_map/while/body/eval_jaxpr/rftj,tk->rfjk/dot_general | solution.py:35
  729.6 22.0 %select_add_fusion.2 = f32[2,2,128,4096]{3,2,1,0:T(8,128)} fusion(f32[2,2,128,4096]{3,2,1,0:T(8,128)} %get-tuple-element.187, pred[]{:T(512)S(6)} %compare.3, s32[256]{0:T(256)S(1)} %add_add_fusion.2, s32[4096]{0:T(1024)S(1)} %iota_add_fusion.2, bf16[2,1,128,256]{2,3,1,0:T(8,128)(2,1)S(1)} %get-tuple-element.177, ...), kind=kOutput, calls=%fused_computation.3.clone.1 | convolution fusion | flops 1089601536 | bytes 17056768 | tf_op jit(solution)/shard_map/while/body/eval_jaxpr/rfjk,tk->rfjt/dot_general | solution.py:45
  751.6 22.2 %fusion.58 = f32[2,2,128,256]{2,3,1,0:T(8,128)S(1)} fusion(bf16[2,2,4096,128]{3,2,1,0:T(8,128)(2,1)} %get-tuple-element.196, s32[256]{0:T(256)S(1)} %add_add_fusion.2, s32[4096]{0:T(1024)S(1)} %iota_add_fusion.2), kind=kOutput, calls=%fused_computation.22.clone.1 | convolution fusion | flops 1085276160 | bytes 4736000 | tf_op jit(solution)/shard_map/while/body/eval_jaxpr/rftj,tk->rfjk/dot_general | solution.py:35
  774.0 22.0 %select_add_fusion.2 = f32[2,2,128,4096]{3,2,1,0:T(8,128)} fusion(f32[2,2,128,4096]{3,2,1,0:T(8,128)} %get-tuple-element.187, pred[]{:T(512)S(6)} %compare.3, s32[256]{0:T(256)S(1)} %add_add_fusion.2, s32[4096]{0:T(1024)S(1)} %iota_add_fusion.2, bf16[2,1,128,256]{2,3,1,0:T(8,128)(2,1)S(1)} %get-tuple-element.177, ...), kind=kOutput, calls=%fused_computation.3.clone.1 | convolution fusion | flops 1089601536 | bytes 17056768 | tf_op jit(solution)/shard_map/while/body/eval_jaxpr/rfjk,tk->rfjt/dot_general | solution.py:45
  796.0 22.2 %fusion.58 = f32[2,2,128,256]{2,3,1,0:T(8,128)S(1)} fusion(bf16[2,2,4096,128]{3,2,1,0:T(8,128)(2,1)} %get-tuple-element.196, s32[256]{0:T(256)S(1)} %add_add_fusion.2, s32[4096]{0:T(1024)S(1)} %iota_add_fusion.2), kind=kOutput, calls=%fused_computation.22.clone.1 | convolution fusion | flops 1085276160 | bytes 4736000 | tf_op jit(solution)/shard_map/while/body/eval_jaxpr/rftj,tk->rfjk/dot_general | solution.py:35
  818.5 22.0 %select_add_fusion.2 = f32[2,2,128,4096]{3,2,1,0:T(8,128)} fusion(f32[2,2,128,4096]{3,2,1,0:T(8,128)} %get-tuple-element.187, pred[]{:T(512)S(6)} %compare.3, s32[256]{0:T(256)S(1)} %add_add_fusion.2, s32[4096]{0:T(1024)S(1)} %iota_add_fusion.2, bf16[2,1,128,256]{2,3,1,0:T(8,128)(2,1)S(1)} %get-tuple-element.177, ...), kind=kOutput, calls=%fused_computation.3.clone.1 | convolution fusion | flops 1089601536 | bytes 17056768 | tf_op jit(solution)/shard_map/while/body/eval_jaxpr/rfjk,tk->rfjt/dot_general | solution.py:45
  840.4 22.2 %fusion.58 = f32[2,2,128,256]{2,3,1,0:T(8,128)S(1)} fusion(bf16[2,2,4096,128]{3,2,1,0:T(8,128)(2,1)} %get-tuple-element.196, s32[256]{0:T(256)S(1)} %add_add_fusion.2, s32[4096]{0:T(1024)S(1)} %iota_add_fusion.2), kind=kOutput, calls=%fused_computation.22.clone.1 | convolution fusion | flops 1085276160 | bytes 4736000 | tf_op jit(solution)/shard_map/while/body/eval_jaxpr/rftj,tk->rfjk/dot_general | solution.py:35
  862.9 22.0 %select_add_fusion.2 = f32[2,2,128,4096]{3,2,1,0:T(8,128)} fusion(f32[2,2,128,4096]{3,2,1,0:T(8,128)} %get-tuple-element.187, pred[]{:T(512)S(6)} %compare.3, s32[256]{0:T(256)S(1)} %add_add_fusion.2, s32[4096]{0:T(1024)S(1)} %iota_add_fusion.2, bf16[2,1,128,256]{2,3,1,0:T(8,128)(2,1)S(1)} %get-tuple-element.177, ...), kind=kOutput, calls=%fused_computation.3.clone.1 | convolution fusion | flops 1089601536 | bytes 17056768 | tf_op jit(solution)/shard_map/while/body/eval_jaxpr/rfjk,tk->rfjt/dot_general | solution.py:45
  884.9 22.2 %fusion.58 = f32[2,2,128,256]{2,3,1,0:T(8,128)S(1)} fusion(bf16[2,2,4096,128]{3,2,1,0:T(8,128)(2,1)} %get-tuple-element.196, s32[256]{0:T(256)S(1)} %add_add_fusion.2, s32[4096]{0:T(1024)S(1)} %iota_add_fusion.2), kind=kOutput, calls=%fused_computation.22.clone.1 | convolution fusion | flops 1085276160 | bytes 4736000 | tf_op jit(solution)/shard_map/while/body/eval_jaxpr/rftj,tk->rfjk/dot_general | solution.py:35
  907.3 22.0 %select_add_fusion.2 = f32[2,2,128,4096]{3,2,1,0:T(8,128)} fusion(f32[2,2,128,4096]{3,2,1,0:T(8,128)} %get-tuple-element.187, pred[]{:T(512)S(6)} %compare.3, s32[256]{0:T(256)S(1)} %add_add_fusion.2, s32[4096]{0:T(1024)S(1)} %iota_add_fusion.2, bf16[2,1,128,256]{2,3,1,0:T(8,128)(2,1)S(1)} %get-tuple-element.177, ...), kind=kOutput, calls=%fused_computation.3.clone.1 | convolution fusion | flops 1089601536 | bytes 17056768 | tf_op jit(solution)/shard_map/while/body/eval_jaxpr/rfjk,tk->rfjt/dot_general | solution.py:45
  929.3 12.4 %copy.23 = bf16[2,2,128,4096]{2,1,0,3:T(2,128)(2,1)} copy(f32[2,2,128,4096]{3,2,1,0:T(8,128)} %get-tuple-element.116) | data formatting | bytes 12582912 | tf_op jit(solution)/shard_map/while | solution.py:50
  954.7 84.4 %all-to-all-done.1 = bf16[2,2,128,4096]{2,1,0,3:T(2,128)(2,1)} async-done(((bf16[2,2,128,4096]{2,1,0,3:T(2,128)(2,1)}), bf16[2,2,128,4096]{2,1,0,3:T(2,128)(2,1)}, u32[]{:S(2)}, u32[]{:S(2)}) %all-to-all-start.1) | async-done | bytes 4194336 | tf_op jit(solution)/shard_map/all_to_all | solution.py:52
  1053.3 14.6 %fusion.33 = f32[2,2,256,2048]{3,2,1,0:T(8,128)} fusion(bf16[2,2,2048,256]{2,3,1,0:T(8,128)(2,1)} %all_to_all.33, bf16[2048,2048]{1,0:T(8,128)(2,1)} %all-gather.2.cloned.1.call-done), kind=kOutput, calls=%fused_computation.42 | convolution fusion | flops 8589934592 | bytes 20971520 | tf_op jit(solution)/shard_map/sj,rfjt->rfts/dot_general | solution.py:53
  1067.9 13.2 %copy.25 = f32[2,2,256,2048]{2,1,3,0:T(2,128)} copy(f32[2,2,256,2048]{3,2,1,0:T(8,128)} %fusion.33) | data formatting | bytes 16777216 | tf_op jit(solution)/shard_map/sj,rfjt->rfts/dot_general | solution.py:53
  1081.1 26.8 %gather_fusion.1 = f32[2048,2,2,256]{3,2,1,0:T(2,128)} fusion(f32[2,2,256,2048]{2,1,3,0:T(2,128)} %copy.25, s32[2048]{0:T(1024)S(1)} %fusion.44), kind=kCustom, calls=%fused_computation.1 | custom fusion | bytes 16785408 | tf_op jit(solution)/shard_map/jit(_take)/gather | solution.py:59
  1107.9 9.8 select_bitcast_fusion
  1117.7 13.1 %copy.26 = f32[2,2,256,2048]{3,2,1,0:T(8,128)} copy(f32[2,2,256,2048]{2,1,0,3:T(2,128)} %select_bitcast_fusion) | data formatting | bytes 16777216 | tf_op jit(solution)/shard_map/jit(_take)/select_n | solution.py:59
  (96 shorter events, 38.8 us)
Async XLA Ops:
  6.5 78.0 %all-gather.2.cloned.1.call-start = ((), (), s32[]{:S(2)}) async-start(), calls=%async_computation.2 | async-start | bytes 8912896 | tf_op jit(solution)/shard_map/all_gather | solution.py:22
  7.3 11.1 copy-start
  109.8 98.7 %all-to-all-start = ((bf16[2,2,256,2048]{2,1,0,3:T(2,128)(2,1)}), bf16[2,2,256,2048]{2,1,0,3:T(2,128)(2,1)}, u32[]{:S(2)}, u32[]{:S(2)}) async-start(bf16[2,2,256,2048]{2,1,0,3:T(2,128)(2,1)} %copy.21), calls=%async_computation | async-start | bytes 8388608 | tf_op jit(solution)/shard_map/all_to_all | solution.py:26
  941.7 97.3 %all-to-all-start.1 = ((bf16[2,2,128,4096]{2,1,0,3:T(2,128)(2,1)}), bf16[2,2,128,4096]{2,1,0,3:T(2,128)(2,1)}, u32[]{:S(2)}, u32[]{:S(2)}) async-start(bf16[2,2,128,4096]{2,1,0,3:T(2,128)(2,1)} %copy.23), calls=%async_computation.1 | async-start | bytes 8388608 | tf_op jit(solution)/shard_map/all_to_all | solution.py:52
Sparse Core Ops, SparseCore 0:
  9.5 74.9 all-gather.1
where the time goes:
time: 1140 us
  matrix products  734 us (64%)
  waiting for transfers between devices  209 us (18%)
  local copies, waits for them, and re-layouts  147 us (13%)
  other arithmetic  23 us (2%)
  between operations  13.4 us (1%)
    dot_general x16, matrix products, one_block(): jnp.einsum('rftj,tk->rfjk', spread, sine_table, preferred_element_type=jn...  355 us
    dot_general x16, matrix products, one_block(): jnp.einsum('rfjk,tk->rfjt', scaled, sine_table, preferred_element_type=jn...  350 us
    all_to_all x1, waiting for transfers between devices, on_device(): lax.all_to_all(modal_data, 'tm', split_axis=3, concat_axis=2, tiled=True)  91.7 us
    all_to_all x1, waiting for transfers between devices, on_device(): lax.all_to_all(back_modes, 'tm', split_axis=3, concat_axis=2, tiled=True)  84.4 us
    all_gather x1, waiting for transfers between devices, on_device(): lax.all_gather(eigenbasis, 'tm', axis=0, tiled=True)  32.3 us
    gather x1, local copies, waits for them, and re-layouts, on_device(): return jnp.take(shaped, inverse, axis=3)  26.8 us
    gather x1, local copies, waits for them, and re-layouts, on_device(): ordered = jnp.take(residual, node_order, axis=3)  24.5 us
  transfers between devices with their start and end apart: 3, of which 3 were waited for; matrix products, arithmetic and copies ran while one was open for 5% of the time, Pallas kernels for 0%

commit v1 on v0

--- a/solution.py
+++ b/solution.py
@@ -2,6 +2,28 @@
 import jax.numpy as jnp
 from jax import lax
 from jax.sharding import PartitionSpec as P
+
+
+def in_order(blocks, dim):
+    blocks = jnp.moveaxis(blocks, 0, dim)
+    lengths = blocks.shape
+    return blocks.reshape(*lengths[:dim], lengths[dim] * lengths[dim + 1], *lengths[dim + 2 :])
+
+
+def collected_by_bits(x, axis):
+    size = lax.axis_size(axis)
+    blocks = x[None]
+    for level in range(size.bit_length() - 1):
+        bit = 1 << level
+        partner_block = lax.ppermute(blocks, axis, [(i, i ^ bit) for i in range(size)])
+        both = jnp.stack([blocks, partner_block])
+        upper = lax.axis_index(axis) >> level & 1
+        blocks = jnp.where(upper == 0, both, both[::-1]).reshape(-1, *x.shape)
+    return blocks
+
+
+def doubled_up(x, axis, dim):
+    return in_order(collected_by_bits(x, axis), dim)
 
 
 def sine_block(length, first_col, block_width):
@@ -19,7 +41,7 @@
     ordered = jnp.take(residual, node_order, axis=3)
     modal_data = jnp.einsum(
         "sj,rfts->rftj",
-        lax.all_gather(eigenbasis, "tm", axis=0, tiled=True),
+        doubled_up(eigenbasis, "tm", 0),
         ordered,
         preferred_element_type=jnp.float32,
     ).astype(jnp.bfloat16)

time: 1140 us -> 1400 us (1.23)
  waiting for transfers between devices: 209 us -> 435 us
  other arithmetic: 23 us -> 51.5 us
    ppermute x0 -> x4, waiting for transfers between devices: none -> 208 us  [collected_by_bits(): lax.ppermute(blocks, axis, [(i, i ^ bit) for i in range(size)])]
    all_to_all x1, waiting for transfers between devices: 91.7 us -> 142 us  [on_device(): lax.all_to_all(modal_data, 'tm', split_axis=3, concat_axis=2, tiled=True)]
    all_gather x1, waiting for transfers between devices: 32.3 us -> 0.01 us  [on_device(): lax.all_gather(eigenbasis, 'tm', axis=0, tiled=True)]
    select_n x0 -> x3, other arithmetic: none -> 17.7 us  [collected_by_bits(): blocks = jnp.where(upper == 0, both, both[::-1]).reshape(-1, *x.shape)]
  transfers between devices with their start and end apart: 3 -> 7, of which waited for: 3 -> 6; matrix products, arithmetic and copies ran while one was open for 5% -> 57% of each run, Pallas kernels for 0% -> 0%
where the time goes in v1:
time: 1400 us; the launch traced here: 1390 us
  matrix products  733 us (52%)
  waiting for transfers between devices  435 us (31%)
  local copies, waits for them, and re-layouts  146 us (10%)
  other arithmetic  51.5 us (4%)
  starting transfers between devices  15.5 us (1%)
    dot_general x16, matrix products, one_block(): jnp.einsum('rftj,tk->rfjk', spread, sine_table, preferred_element_type=jn...  355 us
    dot_general x16, matrix products, one_block(): jnp.einsum('rfjk,tk->rfjt', scaled, sine_table, preferred_element_type=jn...  350 us
    ppermute x4, waiting for transfers between devices, collected_by_bits(): lax.ppermute(blocks, axis, [(i, i ^ bit) for i in range(size)])  208 us
    all_to_all x1, waiting for transfers between devices, on_device(): lax.all_to_all(modal_data, 'tm', split_axis=3, concat_axis=2, tiled=True)  142 us
    all_to_all x1, waiting for transfers between devices, on_device(): lax.all_to_all(back_modes, 'tm', split_axis=3, concat_axis=2, tiled=True)  84.4 us
  transfers between devices with their start and end apart: 7, of which 6 were waited for; matrix products, arithmetic and copies ran while one was open for 57% of the time, Pallas kernels for 0%

profile of v1, /device:TPU:11, one launch (start us, length us, event | category | flops | bytes accessed | tf_op | source)
XLA Modules:
  0.0 1394.5 jit_solution(2115890047581885767)
XLA Ops:
  10.8 24.1 %collective-permute-done.1 = bf16[2,128,2048]{2,1,0:T(8,128)(2,1)S(1)} collective-permute-done((bf16[2,128,2048]{2,1,0:T(8,128)(2,1)S(1)}, bf16[2,128,2048]{2,1,0:T(8,128)(2,1)S(1)}, u32[]{:S(2)}, u32[]{:S(2)}) %collective-permute-start.1) | collective-permute-done | bytes 1048608 | tf_op jit(solution)/shard_map/ppermute | solution.py:18
  35.9 45.9 %collective-permute-done.2 = bf16[4,128,2048]{2,1,0:T(8,128)(2,1)} collective-permute-done((bf16[4,128,2048]{2,1,0:T(8,128)(2,1)S(1)}, bf16[4,128,2048]{2,1,0:T(8,128)(2,1)}, u32[]{:S(2)}, u32[]{:S(2)}) %collective-permute-start.2) | collective-permute-done | bytes 2097184 | tf_op jit(solution)/shard_map/ppermute | solution.py:18
  89.1 11.1 copy.19
  100.3 24.3 %gather_fusion = bf16[2048,2,2,256]{3,2,1,0:T(2,128)(2,1)} fusion(bf16[2,2,256,2048]{2,1,3,0:T(2,128)(2,1)} %copy.19, s32[2048]{0:T(1024)S(1)} %get-tuple-element.147), kind=kCustom, calls=%fused_computation | custom fusion | bytes 8396800 | tf_op jit(solution)/shard_map/jit(_take)/gather | solution.py:41
  133.3 136.2 %collective-permute-done.3 = bf16[8,128,2048]{2,1,0:T(8,128)(2,1)} collective-permute-done((bf16[8,128,2048]{2,1,0:T(8,128)(2,1)}, bf16[8,128,2048]{2,1,0:T(8,128)(2,1)}, u32[]{:S(2)}, u32[]{:S(2)}) %collective-permute-start.3) | collective-permute-done | bytes 4194336 | tf_op jit(solution)/shard_map/ppermute | solution.py:18
  277.1 14.1 %reverse_select_fusion = bf16[2,8,128,2048]{3,2,1,0:T(8,128)(2,1)} fusion(bf16[2,8,128,2048]{3,2,1,0:T(8,128)(2,1)} %pad_maximum_fusion, pred[]{:T(512)S(6)} %eq.20), kind=kLoop, calls=%fused_computation.42 | loop fusion | flops 4194304 | bytes 16777216 | tf_op jit(solution)/shard_map/jit(_where)/select_n | solution.py:21
  291.2 12.7 fusion.38
  304.0 11.1 copy.21
  323.8 141.6 %all-to-all-done = bf16[2,2,256,2048]{2,1,0,3:T(2,128)(2,1)} async-done(((bf16[2,2,256,2048]{2,1,0,3:T(2,128)(2,1)}), bf16[2,2,256,2048]{2,1,0,3:T(2,128)(2,1)}, u32[]{:S(2)}, u32[]{:S(2)}) %all-to-all-start) | async-done | bytes 4194336 | tf_op jit(solution)/shard_map/all_to_all | solution.py:48
  476.4 709.8 %while.16 = (s32[]{:T(128)}, f32[2,2,128,4096]{3,2,1,0:T(8,128)}, f32[128]{0:T(128)S(1)}, bf16[2,2,4096,128]{3,2,1,0:T(8,128)(2,1)}, s32[]{:T(128)}, /*index=5*/s32[]{:T(128)}, s32[]{:T(128)}) while((s32[]{:T(128)}, f32[2,2,128,4096]{3,2,1,0:T(8,128)}, f32[128]{0:T(128)S(1)}, bf16[2,2,4096,128]{3,2,1,0:T(8,128)(2,1)}, s32[]{:T(128)}, ...), condition=%wide.region_2.3_spmd.clone, body=%wide.region_1.2_spmd.clone.sunk | while | flops 2175506432 | bytes 23123560 | solution.py:72
  476.5 22.2 %fusion.58 = f32[2,2,128,256]{2,3,1,0:T(8,128)S(1)} fusion(bf16[2,2,4096,128]{3,2,1,0:T(8,128)(2,1)} %get-tuple-element.198, s32[256]{0:T(256)S(1)} %add_add_fusion.2, s32[4096]{0:T(1024)S(1)} %iota_add_fusion.2), kind=kOutput, calls=%fused_computation.22.clone.1 | convolution fusion | flops 1085276160 | bytes 4736000 | tf_op jit(solution)/shard_map/while/body/eval_jaxpr/rftj,tk->rfjk/dot_general | solution.py:57
  498.9 20.8 %select_add_fusion.2 = f32[2,2,128,4096]{3,2,1,0:T(8,128)} fusion(f32[2,2,128,4096]{3,2,1,0:T(8,128)} %get-tuple-element.189, pred[]{:T(512)S(6)} %compare.3, s32[256]{0:T(256)S(1)} %add_add_fusion.2, s32[4096]{0:T(1024)S(1)} %iota_add_fusion.2, bf16[2,1,128,256]{2,3,1,0:T(8,128)(2,1)S(1)} %get-tuple-element.179, ...), kind=kOutput, calls=%fused_computation.3.clone.1 | convolution fusion | flops 1089601536 | bytes 17056768 | tf_op jit(solution)/shard_map/while/body/eval_jaxpr/rfjk,tk->rfjt/dot_general | solution.py:67
  519.7 22.2 %fusion.58 = f32[2,2,128,256]{2,3,1,0:T(8,128)S(1)} fusion(bf16[2,2,4096,128]{3,2,1,0:T(8,128)(2,1)} %get-tuple-element.198, s32[256]{0:T(256)S(1)} %add_add_fusion.2, s32[4096]{0:T(1024)S(1)} %iota_add_fusion.2), kind=kOutput, calls=%fused_computation.22.clone.1 | convolution fusion | flops 1085276160 | bytes 4736000 | tf_op jit(solution)/shard_map/while/body/eval_jaxpr/rftj,tk->rfjk/dot_general | solution.py:57
  542.2 22.0 %select_add_fusion.2 = f32[2,2,128,4096]{3,2,1,0:T(8,128)} fusion(f32[2,2,128,4096]{3,2,1,0:T(8,128)} %get-tuple-element.189, pred[]{:T(512)S(6)} %compare.3, s32[256]{0:T(256)S(1)} %add_add_fusion.2, s32[4096]{0:T(1024)S(1)} %iota_add_fusion.2, bf16[2,1,128,256]{2,3,1,0:T(8,128)(2,1)S(1)} %get-tuple-element.179, ...), kind=kOutput, calls=%fused_computation.3.clone.1 | convolution fusion | flops 1089601536 | bytes 17056768 | tf_op jit(solution)/shard_map/while/body/eval_jaxpr/rfjk,tk->rfjt/dot_general | solution.py:67
  564.2 22.2 %fusion.58 = f32[2,2,128,256]{2,3,1,0:T(8,128)S(1)} fusion(bf16[2,2,4096,128]{3,2,1,0:T(8,128)(2,1)} %get-tuple-element.198, s32[256]{0:T(256)S(1)} %add_add_fusion.2, s32[4096]{0:T(1024)S(1)} %iota_add_fusion.2), kind=kOutput, calls=%fused_computation.22.clone.1 | convolution fusion | flops 1085276160 | bytes 4736000 | tf_op jit(solution)/shard_map/while/body/eval_jaxpr/rftj,tk->rfjk/dot_general | solution.py:57
  586.6 22.0 %select_add_fusion.2 = f32[2,2,128,4096]{3,2,1,0:T(8,128)} fusion(f32[2,2,128,4096]{3,2,1,0:T(8,128)} %get-tuple-element.189, pred[]{:T(512)S(6)} %compare.3, s32[256]{0:T(256)S(1)} %add_add_fusion.2, s32[4096]{0:T(1024)S(1)} %iota_add_fusion.2, bf16[2,1,128,256]{2,3,1,0:T(8,128)(2,1)S(1)} %get-tuple-element.179, ...), kind=kOutput, calls=%fused_computation.3.clone.1 | convolution fusion | flops 1089601536 | bytes 17056768 | tf_op jit(solution)/shard_map/while/body/eval_jaxpr/rfjk,tk->rfjt/dot_general | solution.py:67
  608.6 22.2 %fusion.58 = f32[2,2,128,256]{2,3,1,0:T(8,128)S(1)} fusion(bf16[2,2,4096,128]{3,2,1,0:T(8,128)(2,1)} %get-tuple-element.198, s32[256]{0:T(256)S(1)} %add_add_fusion.2, s32[4096]{0:T(1024)S(1)} %iota_add_fusion.2), kind=kOutput, calls=%fused_computation.22.clone.1 | convolution fusion | flops 1085276160 | bytes 4736000 | tf_op jit(solution)/shard_map/while/body/eval_jaxpr/rftj,tk->rfjk/dot_general | solution.py:57
  631.1 22.0 %select_add_fusion.2 = f32[2,2,128,4096]{3,2,1,0:T(8,128)} fusion(f32[2,2,128,4096]{3,2,1,0:T(8,128)} %get-tuple-element.189, pred[]{:T(512)S(6)} %compare.3, s32[256]{0:T(256)S(1)} %add_add_fusion.2, s32[4096]{0:T(1024)S(1)} %iota_add_fusion.2, bf16[2,1,128,256]{2,3,1,0:T(8,128)(2,1)S(1)} %get-tuple-element.179, ...), kind=kOutput, calls=%fused_computation.3.clone.1 | convolution fusion | flops 1089601536 | bytes 17056768 | tf_op jit(solution)/shard_map/while/body/eval_jaxpr/rfjk,tk->rfjt/dot_general | solution.py:67
  653.0 22.2 %fusion.58 = f32[2,2,128,256]{2,3,1,0:T(8,128)S(1)} fusion(bf16[2,2,4096,128]{3,2,1,0:T(8,128)(2,1)} %get-tuple-element.198, s32[256]{0:T(256)S(1)} %add_add_fusion.2, s32[4096]{0:T(1024)S(1)} %iota_add_fusion.2), kind=kOutput, calls=%fused_computation.22.clone.1 | convolution fusion | flops 1085276160 | bytes 4736000 | tf_op jit(solution)/shard_map/while/body/eval_jaxpr/rftj,tk->rfjk/dot_general | solution.py:57
  675.5 22.0 %select_add_fusion.2 = f32[2,2,128,4096]{3,2,1,0:T(8,128)} fusion(f32[2,2,128,4096]{3,2,1,0:T(8,128)} %get-tuple-element.189, pred[]{:T(512)S(6)} %compare.3, s32[256]{0:T(256)S(1)} %add_add_fusion.2, s32[4096]{0:T(1024)S(1)} %iota_add_fusion.2, bf16[2,1,128,256]{2,3,1,0:T(8,128)(2,1)S(1)} %get-tuple-element.179, ...), kind=kOutput, calls=%fused_computation.3.clone.1 | convolution fusion | flops 1089601536 | bytes 17056768 | tf_op jit(solution)/shard_map/while/body/eval_jaxpr/rfjk,tk->rfjt/dot_general | solution.py:67
  697.5 22.2 %fusion.58 = f32[2,2,128,256]{2,3,1,0:T(8,128)S(1)} fusion(bf16[2,2,4096,128]{3,2,1,0:T(8,128)(2,1)} %get-tuple-element.198, s32[256]{0:T(256)S(1)} %add_add_fusion.2, s32[4096]{0:T(1024)S(1)} %iota_add_fusion.2), kind=kOutput, calls=%fused_computation.22.clone.1 | convolution fusion | flops 1085276160 | bytes 4736000 | tf_op jit(solution)/shard_map/while/body/eval_jaxpr/rftj,tk->rfjk/dot_general | solution.py:57
  719.9 22.0 %select_add_fusion.2 = f32[2,2,128,4096]{3,2,1,0:T(8,128)} fusion(f32[2,2,128,4096]{3,2,1,0:T(8,128)} %get-tuple-element.189, pred[]{:T(512)S(6)} %compare.3, s32[256]{0:T(256)S(1)} %add_add_fusion.2, s32[4096]{0:T(1024)S(1)} %iota_add_fusion.2, bf16[2,1,128,256]{2,3,1,0:T(8,128)(2,1)S(1)} %get-tuple-element.179, ...), kind=kOutput, calls=%fused_computation.3.clone.1 | convolution fusion | flops 1089601536 | bytes 17056768 | tf_op jit(solution)/shard_map/while/body/eval_jaxpr/rfjk,tk->rfjt/dot_general | solution.py:67
  741.9 22.2 %fusion.58 = f32[2,2,128,256]{2,3,1,0:T(8,128)S(1)} fusion(bf16[2,2,4096,128]{3,2,1,0:T(8,128)(2,1)} %get-tuple-element.198, s32[256]{0:T(256)S(1)} %add_add_fusion.2, s32[4096]{0:T(1024)S(1)} %iota_add_fusion.2), kind=kOutput, calls=%fused_computation.22.clone.1 | convolution fusion | flops 1085276160 | bytes 4736000 | tf_op jit(solution)/shard_map/while/body/eval_jaxpr/rftj,tk->rfjk/dot_general | solution.py:57
  764.4 22.0 %select_add_fusion.2 = f32[2,2,128,4096]{3,2,1,0:T(8,128)} fusion(f32[2,2,128,4096]{3,2,1,0:T(8,128)} %get-tuple-element.189, pred[]{:T(512)S(6)} %compare.3, s32[256]{0:T(256)S(1)} %add_add_fusion.2, s32[4096]{0:T(1024)S(1)} %iota_add_fusion.2, bf16[2,1,128,256]{2,3,1,0:T(8,128)(2,1)S(1)} %get-tuple-element.179, ...), kind=kOutput, calls=%fused_computation.3.clone.1 | convolution fusion | flops 1089601536 | bytes 17056768 | tf_op jit(solution)/shard_map/while/body/eval_jaxpr/rfjk,tk->rfjt/dot_general | solution.py:67
  786.3 22.2 %fusion.58 = f32[2,2,128,256]{2,3,1,0:T(8,128)S(1)} fusion(bf16[2,2,4096,128]{3,2,1,0:T(8,128)(2,1)} %get-tuple-element.198, s32[256]{0:T(256)S(1)} %add_add_fusion.2, s32[4096]{0:T(1024)S(1)} %iota_add_fusion.2), kind=kOutput, calls=%fused_computation.22.clone.1 | convolution fusion | flops 1085276160 | bytes 4736000 | tf_op jit(solution)/shard_map/while/body/eval_jaxpr/rftj,tk->rfjk/dot_general | solution.py:57
  808.8 22.0 %select_add_fusion.2 = f32[2,2,128,4096]{3,2,1,0:T(8,128)} fusion(f32[2,2,128,4096]{3,2,1,0:T(8,128)} %get-tuple-element.189, pred[]{:T(512)S(6)} %compare.3, s32[256]{0:T(256)S(1)} %add_add_fusion.2, s32[4096]{0:T(1024)S(1)} %iota_add_fusion.2, bf16[2,1,128,256]{2,3,1,0:T(8,128)(2,1)S(1)} %get-tuple-element.179, ...), kind=kOutput, calls=%fused_computation.3.clone.1 | convolution fusion | flops 1089601536 | bytes 17056768 | tf_op jit(solution)/shard_map/while/body/eval_jaxpr/rfjk,tk->rfjt/dot_general | solution.py:67
  830.8 22.2 %fusion.58 = f32[2,2,128,256]{2,3,1,0:T(8,128)S(1)} fusion(bf16[2,2,4096,128]{3,2,1,0:T(8,128)(2,1)} %get-tuple-element.198, s32[256]{0:T(256)S(1)} %add_add_fusion.2, s32[4096]{0:T(1024)S(1)} %iota_add_fusion.2), kind=kOutput, calls=%fused_computation.22.clone.1 | convolution fusion | flops 1085276160 | bytes 4736000 | tf_op jit(solution)/shard_map/while/body/eval_jaxpr/rftj,tk->rfjk/dot_general | solution.py:57
  853.3 22.0 %select_add_fusion.2 = f32[2,2,128,4096]{3,2,1,0:T(8,128)} fusion(f32[2,2,128,4096]{3,2,1,0:T(8,128)} %get-tuple-element.189, pred[]{:T(512)S(6)} %compare.3, s32[256]{0:T(256)S(1)} %add_add_fusion.2, s32[4096]{0:T(1024)S(1)} %iota_add_fusion.2, bf16[2,1,128,256]{2,3,1,0:T(8,128)(2,1)S(1)} %get-tuple-element.179, ...), kind=kOutput, calls=%fused_computation.3.clone.1 | convolution fusion | flops 1089601536 | bytes 17056768 | tf_op jit(solution)/shard_map/while/body/eval_jaxpr/rfjk,tk->rfjt/dot_general | solution.py:67
  875.2 22.2 %fusion.58 = f32[2,2,128,256]{2,3,1,0:T(8,128)S(1)} fusion(bf16[2,2,4096,128]{3,2,1,0:T(8,128)(2,1)} %get-tuple-element.198, s32[256]{0:T(256)S(1)} %add_add_fusion.2, s32[4096]{0:T(1024)S(1)} %iota_add_fusion.2), kind=kOutput, calls=%fused_computation.22.clone.1 | convolution fusion | flops 1085276160 | bytes 4736000 | tf_op jit(solution)/shard_map/while/body/eval_jaxpr/rftj,tk->rfjk/dot_general | solution.py:57
  897.7 22.0 %select_add_fusion.2 = f32[2,2,128,4096]{3,2,1,0:T(8,128)} fusion(f32[2,2,128,4096]{3,2,1,0:T(8,128)} %get-tuple-element.189, pred[]{:T(512)S(6)} %compare.3, s32[256]{0:T(256)S(1)} %add_add_fusion.2, s32[4096]{0:T(1024)S(1)} %iota_add_fusion.2, bf16[2,1,128,256]{2,3,1,0:T(8,128)(2,1)S(1)} %get-tuple-element.179, ...), kind=kOutput, calls=%fused_computation.3.clone.1 | convolution fusion | flops 1089601536 | bytes 17056768 | tf_op jit(solution)/shard_map/while/body/eval_jaxpr/rfjk,tk->rfjt/dot_general | solution.py:67
  919.7 22.2 %fusion.58 = f32[2,2,128,256]{2,3,1,0:T(8,128)S(1)} fusion(bf16[2,2,4096,128]{3,2,1,0:T(8,128)(2,1)} %get-tuple-element.198, s32[256]{0:T(256)S(1)} %add_add_fusion.2, s32[4096]{0:T(1024)S(1)} %iota_add_fusion.2), kind=kOutput, calls=%fused_computation.22.clone.1 | convolution fusion | flops 1085276160 | bytes 4736000 | tf_op jit(solution)/shard_map/while/body/eval_jaxpr/rftj,tk->rfjk/dot_general | solution.py:57
  942.1 22.0 %select_add_fusion.2 = f32[2,2,128,4096]{3,2,1,0:T(8,128)} fusion(f32[2,2,128,4096]{3,2,1,0:T(8,128)} %get-tuple-element.189, pred[]{:T(512)S(6)} %compare.3, s32[256]{0:T(256)S(1)} %add_add_fusion.2, s32[4096]{0:T(1024)S(1)} %iota_add_fusion.2, bf16[2,1,128,256]{2,3,1,0:T(8,128)(2,1)S(1)} %get-tuple-element.179, ...), kind=kOutput, calls=%fused_computation.3.clone.1 | convolution fusion | flops 1089601536 | bytes 17056768 | tf_op jit(solution)/shard_map/while/body/eval_jaxpr/rfjk,tk->rfjt/dot_general | solution.py:67
  964.1 22.2 %fusion.58 = f32[2,2,128,256]{2,3,1,0:T(8,128)S(1)} fusion(bf16[2,2,4096,128]{3,2,1,0:T(8,128)(2,1)} %get-tuple-element.198, s32[256]{0:T(256)S(1)} %add_add_fusion.2, s32[4096]{0:T(1024)S(1)} %iota_add_fusion.2), kind=kOutput, calls=%fused_computation.22.clone.1 | convolution fusion | flops 1085276160 | bytes 4736000 | tf_op jit(solution)/shard_map/while/body/eval_jaxpr/rftj,tk->rfjk/dot_general | solution.py:57
  986.6 22.0 %select_add_fusion.2 = f32[2,2,128,4096]{3,2,1,0:T(8,128)} fusion(f32[2,2,128,4096]{3,2,1,0:T(8,128)} %get-tuple-element.189, pred[]{:T(512)S(6)} %compare.3, s32[256]{0:T(256)S(1)} %add_add_fusion.2, s32[4096]{0:T(1024)S(1)} %iota_add_fusion.2, bf16[2,1,128,256]{2,3,1,0:T(8,128)(2,1)S(1)} %get-tuple-element.179, ...), kind=kOutput, calls=%fused_computation.3.clone.1 | convolution fusion | flops 1089601536 | bytes 17056768 | tf_op jit(solution)/shard_map/while/body/eval_jaxpr/rfjk,tk->rfjt/dot_general | solution.py:67
  1008.5 22.2 %fusion.58 = f32[2,2,128,256]{2,3,1,0:T(8,128)S(1)} fusion(bf16[2,2,4096,128]{3,2,1,0:T(8,128)(2,1)} %get-tuple-element.198, s32[256]{0:T(256)S(1)} %add_add_fusion.2, s32[4096]{0:T(1024)S(1)} %iota_add_fusion.2), kind=kOutput, calls=%fused_computation.22.clone.1 | convolution fusion | flops 1085276160 | bytes 4736000 | tf_op jit(solution)/shard_map/while/body/eval_jaxpr/rftj,tk->rfjk/dot_general | solution.py:57
  1031.0 22.0 %select_add_fusion.2 = f32[2,2,128,4096]{3,2,1,0:T(8,128)} fusion(f32[2,2,128,4096]{3,2,1,0:T(8,128)} %get-tuple-element.189, pred[]{:T(512)S(6)} %compare.3, s32[256]{0:T(256)S(1)} %add_add_fusion.2, s32[4096]{0:T(1024)S(1)} %iota_add_fusion.2, bf16[2,1,128,256]{2,3,1,0:T(8,128)(2,1)S(1)} %get-tuple-element.179, ...), kind=kOutput, calls=%fused_computation.3.clone.1 | convolution fusion | flops 1089601536 | bytes 17056768 | tf_op jit(solution)/shard_map/while/body/eval_jaxpr/rfjk,tk->rfjt/dot_general | solution.py:67
  1053.0 22.2 %fusion.58 = f32[2,2,128,256]{2,3,1,0:T(8,128)S(1)} fusion(bf16[2,2,4096,128]{3,2,1,0:T(8,128)(2,1)} %get-tuple-element.198, s32[256]{0:T(256)S(1)} %add_add_fusion.2, s32[4096]{0:T(1024)S(1)} %iota_add_fusion.2), kind=kOutput, calls=%fused_computation.22.clone.1 | convolution fusion | flops 1085276160 | bytes 4736000 | tf_op jit(solution)/shard_map/while/body/eval_jaxpr/rftj,tk->rfjk/dot_general | solution.py:57
  1075.4 22.0 %select_add_fusion.2 = f32[2,2,128,4096]{3,2,1,0:T(8,128)} fusion(f32[2,2,128,4096]{3,2,1,0:T(8,128)} %get-tuple-element.189, pred[]{:T(512)S(6)} %compare.3, s32[256]{0:T(256)S(1)} %add_add_fusion.2, s32[4096]{0:T(1024)S(1)} %iota_add_fusion.2, bf16[2,1,128,256]{2,3,1,0:T(8,128)(2,1)S(1)} %get-tuple-element.179, ...), kind=kOutput, calls=%fused_computation.3.clone.1 | convolution fusion | flops 1089601536 | bytes 17056768 | tf_op jit(solution)/shard_map/while/body/eval_jaxpr/rfjk,tk->rfjt/dot_general | solution.py:67
  1097.4 22.2 %fusion.58 = f32[2,2,128,256]{2,3,1,0:T(8,128)S(1)} fusion(bf16[2,2,4096,128]{3,2,1,0:T(8,128)(2,1)} %get-tuple-element.198, s32[256]{0:T(256)S(1)} %add_add_fusion.2, s32[4096]{0:T(1024)S(1)} %iota_add_fusion.2), kind=kOutput, calls=%fused_computation.22.clone.1 | convolution fusion | flops 1085276160 | bytes 4736000 | tf_op jit(solution)/shard_map/while/body/eval_jaxpr/rftj,tk->rfjk/dot_general | solution.py:57
  1119.9 22.0 %select_add_fusion.2 = f32[2,2,128,4096]{3,2,1,0:T(8,128)} fusion(f32[2,2,128,4096]{3,2,1,0:T(8,128)} %get-tuple-element.189, pred[]{:T(512)S(6)} %compare.3, s32[256]{0:T(256)S(1)} %add_add_fusion.2, s32[4096]{0:T(1024)S(1)} %iota_add_fusion.2, bf16[2,1,128,256]{2,3,1,0:T(8,128)(2,1)S(1)} %get-tuple-element.179, ...), kind=kOutput, calls=%fused_computation.3.clone.1 | convolution fusion | flops 1089601536 | bytes 17056768 | tf_op jit(solution)/shard_map/while/body/eval_jaxpr/rfjk,tk->rfjt/dot_general | solution.py:67
  1141.9 22.2 %fusion.58 = f32[2,2,128,256]{2,3,1,0:T(8,128)S(1)} fusion(bf16[2,2,4096,128]{3,2,1,0:T(8,128)(2,1)} %get-tuple-element.198, s32[256]{0:T(256)S(1)} %add_add_fusion.2, s32[4096]{0:T(1024)S(1)} %iota_add_fusion.2), kind=kOutput, calls=%fused_computation.22.clone.1 | convolution fusion | flops 1085276160 | bytes 4736000 | tf_op jit(solution)/shard_map/while/body/eval_jaxpr/rftj,tk->rfjk/dot_general | solution.py:57
  1164.3 22.0 %select_add_fusion.2 = f32[2,2,128,4096]{3,2,1,0:T(8,128)} fusion(f32[2,2,128,4096]{3,2,1,0:T(8,128)} %get-tuple-element.189, pred[]{:T(512)S(6)} %compare.3, s32[256]{0:T(256)S(1)} %add_add_fusion.2, s32[4096]{0:T(1024)S(1)} %iota_add_fusion.2, bf16[2,1,128,256]{2,3,1,0:T(8,128)(2,1)S(1)} %get-tuple-element.179, ...), kind=kOutput, calls=%fused_computation.3.clone.1 | convolution fusion | flops 1089601536 | bytes 17056768 | tf_op jit(solution)/shard_map/while/body/eval_jaxpr/rfjk,tk->rfjt/dot_general | solution.py:67
  1186.3 12.5 copy.23
  1211.6 84.4 %all-to-all-done.1 = bf16[2,2,128,4096]{2,1,0,3:T(2,128)(2,1)} async-done(((bf16[2,2,128,4096]{2,1,0,3:T(2,128)(2,1)}), bf16[2,2,128,4096]{2,1,0,3:T(2,128)(2,1)}, u32[]{:S(2)}, u32[]{:S(2)}) %all-to-all-start.1) | async-done | bytes 4194336 | tf_op jit(solution)/shard_map/all_to_all | solution.py:74
  1310.2 14.6 %fusion.33 = f32[2,2,256,2048]{3,2,1,0:T(8,128)} fusion(bf16[2,2,2048,256]{2,3,1,0:T(8,128)(2,1)} %all_to_all.33, bf16[2048,2048]{1,0:T(8,128)(2,1)} %all-gather.2.cloned.1.call-done), kind=kOutput, calls=%fused_computation.44 | convolution fusion | flops 8589934592 | bytes 20971520 | tf_op jit(solution)/shard_map/sj,rfjt->rfts/dot_general | solution.py:75
  1324.7 13.2 copy.25
  1337.9 26.8 %gather_fusion.1 = f32[2048,2,2,256]{3,2,1,0:T(2,128)} fusion(f32[2,2,256,2048]{2,1,3,0:T(2,128)} %copy.25, s32[2048]{0:T(1024)S(1)} %fusion.43), kind=kCustom, calls=%fused_computation.1 | custom fusion | bytes 16785408 | tf_op jit(solution)/shard_map/jit(_take)/gather | solution.py:81
  1374.5 13.1 copy.26
  (112 shorter events, 89.3 us)
Async XLA Ops:
  6.5 2.4 collective-permute-start
  10.5 24.4 %collective-permute-start.1 = (bf16[2,128,2048]{2,1,0:T(8,128)(2,1)S(1)}, bf16[2,128,2048]{2,1,0:T(8,128)(2,1)S(1)}, u32[]{:S(2)}, u32[]{:S(2)}) collective-permute-start(bf16[2,128,2048]{2,1,0:T(8,128)(2,1)S(1)} %get-tuple-element.145), channel_id=1, source_target_pairs={{0,2},{1,3},{2,0},{3,1},{4,6},{5,7},{6,4},{7,5},{8,10},{9,11},{10,... | collective-permute-start | bytes 3145736 | tf_op jit(solution)/shard_map/ppermute | solution.py:18
  35.6 46.1 %collective-permute-start.2 = (bf16[4,128,2048]{2,1,0:T(8,128)(2,1)S(1)}, bf16[4,128,2048]{2,1,0:T(8,128)(2,1)}, u32[]{:S(2)}, u32[]{:S(2)}) collective-permute-start(bf16[4,128,2048]{2,1,0:T(8,128)(2,1)S(1)} %bitcast.64), channel_id=1, source_target_pairs={{0,4},{1,5},{2,6},{3,7},{4,0},{5,1},{6,2},{7,3},{8,12},{9,13},{10,... | collective-permute-start | bytes 6291464 | tf_op jit(solution)/shard_map/ppermute | solution.py:18
  86.8 182.7 %collective-permute-start.3 = (bf16[8,128,2048]{2,1,0:T(8,128)(2,1)}, bf16[8,128,2048]{2,1,0:T(8,128)(2,1)}, u32[]{:S(2)}, u32[]{:S(2)}) collective-permute-start(bf16[8,128,2048]{2,1,0:T(8,128)(2,1)} %bitcast.11), channel_id=1, source_target_pairs={{0,8},{1,9},{2,10},{3,11},{4,12},{5,13},{6,14},{7,15},{8,0},{9,1},... | collective-permute-start | bytes 12582920 | tf_op jit(solution)/shard_map/ppermute | solution.py:18
  89.1 11.1 copy-start
  315.1 150.3 %all-to-all-start = ((bf16[2,2,256,2048]{2,1,0,3:T(2,128)(2,1)}), bf16[2,2,256,2048]{2,1,0,3:T(2,128)(2,1)}, u32[]{:S(2)}, u32[]{:S(2)}) async-start(bf16[2,2,256,2048]{2,1,0,3:T(2,128)(2,1)} %copy.21), calls=%async_computation | async-start | bytes 8388608 | tf_op jit(solution)/shard_map/all_to_all | solution.py:48
  322.3 987.9 %all-gather.2.cloned.1.call-start = ((), (), s32[]{:S(2)}) async-start(), calls=%async_computation.2 | async-start | bytes 8912896 | tf_op jit(solution)/shard_map/all_gather | solution.py:77
  1198.7 97.2 %all-to-all-start.1 = ((bf16[2,2,128,4096]{2,1,0,3:T(2,128)(2,1)}), bf16[2,2,128,4096]{2,1,0,3:T(2,128)(2,1)}, u32[]{:S(2)}, u32[]{:S(2)}) async-start(bf16[2,2,128,4096]{2,1,0,3:T(2,128)(2,1)} %copy.23), calls=%async_computation.1 | async-start | bytes 8388608 | tf_op jit(solution)/shard_map/all_to_all | solution.py:74
Sparse Core Ops, SparseCore 0:
  325.3 127.2 all-gather.1
